TPU v7x, 512 devices: a whole 4x4x16 slice. The times are simulated.
512 devices in a mesh: row: 16 (over z_lo, core), col: 32 (over x, y, z_hi).
Axes of the slice: x: 4, y: 4, z: 16 (z_hi: 2, z_lo: 8; z = z_hi * 8 + z_lo), core: 2. Of those that a mesh axis runs over, the one named last changes fastest.
Arguments:
- greens: float32 [13824, 13824], P('row', 'col')
- accepted_sites: int32 [256], replicated, may hold values from 0 to 13823, as said below
- field_values: int32 [256], replicated, may hold values from -1 to 1, as said below
- left_a: float32 [96, 144, 144], P('row')
- left_b: float32 [96, 144, 144], P('row')
- right_a: float32 [96, 144, 144], P('col')
- right_b: float32 [96, 144, 144], P('col')
Outputs:
- wrapped: float32 [13824, 13824], P('row', 'col')
Inputs may be any that keep to these rules, and one draw needn't show every extreme that they name: `accepted_sites`: site k (from 0) lies in [k * 54, (k + 1) * 54), so the sites rise. `field_values`: each value is -1 or 1.
All inputs are finite; a program needn't handle non-finite values.
Results may differ from a plain program's by a relative error of at most 0.000073.
Values sent between devices are 32-bit elements; how exact they have to be, the bound alone decides.
A program may use at most 64 MiB of HBM per device.

v0:
```python
import jax
import jax.numpy as jnp
from jax import lax
from jax.sharding import PartitionSpec as P

highest = lax.Precision.HIGHEST
coupling = 0.45


def padded_2(x, sides, width):
    for axis, dim in sides:
        size, length = (lax.axis_size(axis), x.shape[dim])
        up = [(i, (i + 1) % size) for i in range(size)]
        down = [(j, i) for i, j in up]
        last = lax.slice_in_dim(x, length - width, length, axis=dim)
        leading = lax.slice_in_dim(x, 0, width, axis=dim)
        before = lax.ppermute(last, axis, up)
        after = lax.ppermute(leading, axis, down)
        x = jnp.concatenate([before, x, after], axis=dim)
    return x


def from_behind(value, axis, steps):
    count = lax.axis_size(axis)
    pairs = [(source, (source + steps) % count) for source in range(count)]
    return lax.ppermute(value, axis, pairs)


def blocks_left(blocks, matrix):
    number = blocks.shape[0]
    cluster = blocks.shape[1]
    product = jnp.einsum(
        "cab,cbm->cam", blocks, matrix.reshape(number, cluster, matrix.shape[1]), precision=highest
    )
    return product.reshape(number * cluster, matrix.shape[1])


def blocks_right(matrix, blocks):
    number = blocks.shape[0]
    cluster = blocks.shape[1]
    product = jnp.einsum(
        "mcb,cba->mca", matrix.reshape(matrix.shape[0], number, cluster), blocks, precision=highest
    )
    return product.reshape(matrix.shape[0], number * cluster)


def left_apply(matrix, first_blocks, second_blocks, carried):
    height = matrix.shape[0]
    margin = first_blocks.shape[1] // 2
    inner = blocks_left(first_blocks, matrix)
    padded = padded_2(inner, (("row", 0),), margin)
    stacked = jnp.concatenate([carried[None], second_blocks], axis=0)
    return blocks_left(stacked, padded)[margin : margin + height]


def right_apply(matrix, first_blocks, second_blocks, carried):
    breadth = matrix.shape[1]
    margin = first_blocks.shape[1] // 2
    inner = blocks_right(matrix, first_blocks)
    padded = padded_2(inner, (("col", 1),), margin)
    stacked = jnp.concatenate([carried[None], second_blocks], axis=0)
    return blocks_right(padded, stacked)[:, margin : margin + breadth]


def whole_apply(matrix, left_a, left_b, right_a, right_b, carried_left, carried_right):
    left_done = left_apply(matrix, left_a, left_b, carried_left)
    return right_apply(left_done, right_a, right_b, carried_right)


def on_device(greens, accepted_sites, field_values, left_a, left_b, right_a, right_b):
    height = greens.shape[0]
    breadth = greens.shape[1]
    accepted = accepted_sites.shape[0]
    row_base = lax.axis_index("row") * height
    col_base = lax.axis_index("col") * breadth
    col_hit = (
        accepted_sites[None, :]
        == col_base + lax.broadcasted_iota(jnp.int32, (breadth, accepted), 0)
    ).astype(jnp.float32)
    row_hit = (
        accepted_sites[:, None] == row_base + lax.broadcasted_iota(jnp.int32, (accepted, height), 1)
    ).astype(jnp.float32)
    g_cols = lax.psum(jnp.dot(greens, col_hit, precision=highest), "col")
    g_rows = lax.psum(jnp.dot(row_hit, greens, precision=highest), "row")
    g_pair = lax.psum(jnp.dot(g_rows, col_hit, precision=highest), "col")
    shifts = jnp.exp(-2.0 * coupling * field_values.astype(jnp.float32)) - 1.0
    identity = jnp.eye(accepted, dtype=jnp.float32)
    capacity = identity + (identity - g_pair) * shifts[None, :]
    normal_matrix = jnp.dot(capacity.T, capacity, precision=highest)
    lower_factor = jnp.linalg.cholesky(normal_matrix)
    middle = lax.linalg.triangular_solve(lower_factor, capacity.T, left_side=True, lower=True)
    inverse = lax.linalg.triangular_solve(
        lower_factor, middle, left_side=True, lower=True, transpose_a=True
    )
    scaled = shifts[:, None] * inverse
    complement = col_hit.T - g_rows
    factor = jnp.dot(scaled, complement, precision=highest)
    carried_left = from_behind(left_b[-1], "row", 1)
    carried_right = from_behind(right_b[-1], "col", 1)
    updated = greens - jnp.dot(g_cols, factor, precision=highest)
    return whole_apply(updated, left_a, left_b, right_a, right_b, carried_left, carried_right)


def solution(mesh):
    return jax.shard_map(
        on_device,
        mesh=mesh,
        in_specs=(
            P("row", "col"),
            P(),
            P(),
            P("row", None, None),
            P("row", None, None),
            P("col", None, None),
            P("col", None, None),
        ),
        out_specs=P("row", "col"),
        check_vma=False,
    )
```

profile of v0, /device:TPU:0, one launch (start us, length us, event | category | flops | bytes accessed | tf_op | source)
XLA Modules:
  0.0 1041.7 jit_solution(11595491443462869906)
XLA Ops:
  6.6 3.4 fusion.4
  10.1 2.1 convolution_bitcast_fusion
  12.2 190.4 %all-reduce.5.cloned.1.call-done = f32[256,432]{0,1:T(8,128)} async-done(((f32[256,432]{0,1:T(8,128)}), f32[256,432]{0,1:T(8,128)}) %all-reduce.5.cloned.1.call-update) | async-done | bytes 442384 | tf_op jit(solution)/shard_map/psum | solution.py:84
  202.5 2.4 fusion.10
  205.0 634.1 %all-reduce.7.cloned.1.call-done = (f32[864,256]{0,1:T(8,128)}, f32[256,256]{1,0:T(8,128)}) async-done(((f32[864,256]{0,1:T(8,128)}, f32[256,256]{1,0:T(8,128)}), (f32[864,256]{0,1:T(8,128)}, f32[256,256]{1,0:T(8,128)})) %all-reduce.7.cloned.1.call-update) | async-done | bytes 1146896 | tf_op jit(solution)/shard_map/psum | solution.py:83
  843.4 11.7 %cholesky.50 = f32[128,128]{1,0:T(8,128)S(1)} custom-call(f32[128,128]{1,0:T(8,128)S(1)} %cholesky.118), custom_call_target="Cholesky" | custom-call | tf_op jit(solution)/shard_map/jit(cholesky)/cholesky | solution.py:90
  855.1 9.8 custom-call.16
  867.1 11.9 %cholesky.105 = f32[128,128]{1,0:T(8,128)S(1)} custom-call(f32[128,128]{1,0:T(8,128)S(1)} %convolution_subtract_fusion.3), custom_call_target="Cholesky" | custom-call | tf_op jit(solution)/shard_map/jit(cholesky)/cholesky | solution.py:90
  881.1 4.0 while.1
  885.1 19.7 %custom-call.17 = f32[2,128,128]{1,2,0:T(8,128)S(1)} custom-call(f32[2,128,128]{2,1,0:T(8,128)S(1)} %get-tuple-element.12), custom_call_target="InvertDiagBlocksLowerTriangular" | custom-call | tf_op jit(solution)/shard_map/triangular_solve | solution.py:92
  909.3 2.8 convolution_subtract_fusion
  912.1 2.1 copy.17
  914.2 1.7 fusion.49
  916.0 1.9 collective-permute-start.2
  917.9 10.2 collective-permute-start.3
  928.2 2.1 collective-permute-start.1
  931.0 10.2 collective-permute-done.1
  941.3 1.9 fusion
  945.1 3.1 fusion.50
  949.0 14.2 %collective-permute-start.4 = (f32[864,72]{0,1:T(8,128)}, f32[864,72]{0,1:T(8,128)}, u32[]{:S(2)}, u32[]{:S(2)}) collective-permute-start(f32[864,72]{0,1:T(8,128)} %get-tuple-element.27), channel_id=1, source_target_pairs={{0,1},{1,2},{2,3},{3,4},{4,5},{5,6},{6,7},{7,8},{8,9},{9,10},{10,1... | collective-permute-start | bytes 746504 | tf_op jit(solution)/shard_map/ppermute | solution.py:17
  963.2 48.1 %collective-permute-start.5 = (f32[864,72]{0,1:T(8,128)}, f32[864,72]{0,1:T(8,128)}, u32[]{:S(2)}, u32[]{:S(2)}) collective-permute-start(f32[864,72]{0,1:T(8,128)} %get-tuple-element.28), channel_id=1, source_target_pairs={{1,0},{2,1},{3,2},{4,3},{5,4},{6,5},{7,6},{8,7},{9,8},{10,9},{11,1... | collective-permute-start | bytes 746504 | tf_op jit(solution)/shard_map/ppermute | solution.py:18
  1011.6 1.9 collective-permute-start
  1016.7 14.9 %collective-permute-done = f32[144,144]{0,1:T(8,128)S(1)} collective-permute-done((f32[144,144]{0,1:T(8,128)S(1)}, f32[144,144]{0,1:T(8,128)S(1)}, u32[]{:S(2)}, u32[]{:S(2)}) %collective-permute-start) | collective-permute-done | bytes 82976 | tf_op jit(solution)/shard_map/ppermute | solution.py:26
  1031.5 2.1 fusion.6
  (69 shorter events, 23.8 us)
Async XLA Ops:
  6.5 907.6 %copy-start = (f32[6,144,144]{2,1,0:T(8,128)S(1)}, f32[6,144,144]{2,1,0:T(8,128)}, u32[]{:S(2)}) copy-start(f32[6,144,144]{2,1,0:T(8,128)} %param.10) | copy-start | bytes 1492996
  6.5 3.5 copy-start.1
  6.5 3.5 copy-start.8
  6.5 196.0 %all-reduce.5.cloned.1.call-start = ((), (), s32[]{:S(2)}) async-start(), calls=%async_computation | async-start | bytes 884736 | tf_op jit(solution)/shard_map/psum | solution.py:84
  10.0 829.2 %all-reduce.7.cloned.1.call-start = ((), (), s32[]{:S(2)}) async-start(), calls=%async_computation.1 | async-start | bytes 2359296 | tf_op jit(solution)/shard_map/psum | solution.py:83
  10.1 194.9 %copy-start.9 = (s32[256]{0:T(256)S(1)}, s32[256]{0:T(256)}, u32[]{:S(2)}) copy-start(s32[256]{0:T(256)} %param.9) | copy-start | bytes 3076
  842.7 0.7 copy-start.5
  881.0 27.6 %copy-start.2 = (f32[256,432]{0,1:T(8,128)S(1)}, f32[256,432]{0,1:T(8,128)}, u32[]{:S(2)}) copy-start(f32[256,432]{0,1:T(8,128)} %all-reduce.5.cloned.1.call-done) | copy-start | bytes 1327108
  904.8 4.5 copy-start.4
  914.2 14.0 %copy-start.3 = (f32[6,144,144]{2,1,0:T(8,128)S(1)}, f32[6,144,144]{2,1,0:T(8,128)}, u32[]{:S(2)}) copy-start(f32[6,144,144]{2,1,0:T(8,128)} %param.11) | copy-start | bytes 1492996
  916.0 14.4 %collective-permute-start.2 = (f32[72,432]{1,0:T(8,128)S(1)}, f32[72,432]{1,0:T(8,128)S(1)}, u32[]{:S(2)}, u32[]{:S(2)}) collective-permute-start(f32[72,432]{1,0:T(8,128)S(1)} %get-tuple-element.25), channel_id=1, source_target_pairs={{0,32},{32,64},{64,96},{96,128},{128,160},{160,192},{192,224},{224... | collective-permute-start | bytes 373256 | tf_op jit(solution)/shard_map/ppermute | solution.py:17
  917.9 12.9 %collective-permute-start.3 = (f32[72,432]{1,0:T(8,128)S(1)}, f32[72,432]{1,0:T(8,128)S(1)}, u32[]{:S(2)}, u32[]{:S(2)}) collective-permute-start(f32[72,432]{1,0:T(8,128)S(1)} %get-tuple-element.26), channel_id=1, source_target_pairs={{32,0},{64,32},{96,64},{128,96},{160,128},{192,160},{224,192},{256... | collective-permute-start | bytes 373256 | tf_op jit(solution)/shard_map/ppermute | solution.py:18
  928.2 13.1 %collective-permute-start.1 = (f32[144,144]{1,0:T(8,128)S(1)}, f32[144,144]{1,0:T(8,128)S(1)}, u32[]{:S(2)}, u32[]{:S(2)}) collective-permute-start(f32[144,144]{1,0:T(8,128)S(1)} %slice_bitcast_fusion.1), channel_id=1, source_target_pairs={{0,32},{32,64},{64,96},{96,128},{128,160},{160,192},{192,224},{224... | collective-permute-start | bytes 248840 | tf_op jit(solution)/shard_map/ppermute | solution.py:26
  943.3 1.7 copy-start.6
  945.1 66.3 %copy-start.7 = (f32[3,144,144]{2,1,0:T(8,128)S(1)}, f32[3,144,144]{2,1,0:T(8,128)}, u32[]{:S(2)}) copy-start(f32[3,144,144]{2,1,0:T(8,128)} %param.13) | copy-start | bytes 746500
  949.0 65.0 %collective-permute-start.4 = (f32[864,72]{0,1:T(8,128)}, f32[864,72]{0,1:T(8,128)}, u32[]{:S(2)}, u32[]{:S(2)}) collective-permute-start(f32[864,72]{0,1:T(8,128)} %get-tuple-element.27), channel_id=1, source_target_pairs={{0,1},{1,2},{2,3},{3,4},{4,5},{5,6},{6,7},{7,8},{8,9},{9,10},{10,1... | collective-permute-start | bytes 746504 | tf_op jit(solution)/shard_map/ppermute | solution.py:17
  963.2 52.2 %collective-permute-start.5 = (f32[864,72]{0,1:T(8,128)}, f32[864,72]{0,1:T(8,128)}, u32[]{:S(2)}, u32[]{:S(2)}) collective-permute-start(f32[864,72]{0,1:T(8,128)} %get-tuple-element.28), channel_id=1, source_target_pairs={{1,0},{2,1},{3,2},{4,3},{5,4},{6,5},{7,6},{8,7},{9,8},{10,9},{11,1... | collective-permute-start | bytes 746504 | tf_op jit(solution)/shard_map/ppermute | solution.py:18
  1011.6 20.0 %collective-permute-start = (f32[144,144]{0,1:T(8,128)S(1)}, f32[144,144]{0,1:T(8,128)S(1)}, u32[]{:S(2)}, u32[]{:S(2)}) collective-permute-start(f32[144,144]{0,1:T(8,128)S(1)} %slice_bitcast_fusion), channel_id=1, source_target_pairs={{0,1},{1,2},{2,3},{3,4},{4,5},{5,6},{6,7},{7,8},{8,9},{9,10},{10,1... | collective-permute-start | bytes 248840 | tf_op jit(solution)/shard_map/ppermute | solution.py:26
Sparse Core Ops, SparseCore 0:
  10.3 192.2 all-reduce.4
  205.8 633.3 all-reduce.6
where the time goes:
time: 1040 us
  waiting for transfers between devices  852 us (82%)
  starting transfers between devices  78.5 us (8%)
  other arithmetic  57 us (5%)
  matrix products  27.8 us (3%)
  between operations  15.1 us (1%)
  local copies, waits for them, and re-layouts  11.1 us (1%)
    psum x1, waiting for transfers between devices, on_device(): g_cols = lax.psum(jnp.dot(greens, col_hit, precision=highest), 'col')  634 us
    psum x1, waiting for transfers between devices, on_device(): g_rows = lax.psum(jnp.dot(row_hit, greens, precision=highest), 'row')  190 us
    ppermute x2, starting transfers between devices, padded_2(): after = lax.ppermute(leading, axis, down)  58.3 us
    another operation x6, other arithmetic, on_device(): lower_factor = jnp.linalg.cholesky(normal_matrix)  34.2 us
    ppermute x2, waiting for transfers between devices, from_behind(): return lax.ppermute(value, axis, pairs)  25.1 us
  transfers between devices with their start and end apart: 8, of which 7 were waited for; matrix products, arithmetic and copies ran while one was open for 0% of the time, Pallas kernels for 0%

commit v1 on v0

--- a/solution.py
+++ b/solution.py
@@ -81,7 +81,7 @@
         accepted_sites[:, None] == row_base + lax.broadcasted_iota(jnp.int32, (accepted, height), 1)
     ).astype(jnp.float32)
     g_cols = lax.psum(jnp.dot(greens, col_hit, precision=highest), "col")
-    g_rows = lax.psum(jnp.dot(row_hit, greens, precision=highest), "row")
+    g_rows = jnp.sum(lax.all_gather(jnp.dot(row_hit, greens, precision=highest), "row"), axis=0)
     g_pair = lax.psum(jnp.dot(g_rows, col_hit, precision=highest), "col")
     shifts = jnp.exp(-2.0 * coupling * field_values.astype(jnp.float32)) - 1.0
     identity = jnp.eye(accepted, dtype=jnp.float32)

time: 1040 us -> 966 us (0.929)
  waiting for transfers between devices: 852 us -> 767 us
    psum x1 -> x0, waiting for transfers between devices: 190 us -> none  [on_device(): g_rows = lax.psum(jnp.dot(row_hit, greens, precision=highest), 'row')]
    all_gather x0 -> x1, waiting for transfers between devices: none -> 111 us  [on_device(): lax.all_gather(jnp.dot(row_hit, greens, precision=highest), 'row')]
    ppermute x2, starting transfers between devices: 58.3 us -> 22.1 us  [padded_2(): after = lax.ppermute(leading, axis, down)]
    ppermute x2, starting transfers between devices: 16.1 us -> 49.7 us  [padded_2(): before = lax.ppermute(last, axis, up)]
  transfers between devices with their start and end apart: 8 -> 8, of which waited for: 7 -> 6; matrix products, arithmetic and copies ran while one was open for 0% -> 0% of each run, Pallas kernels for 0% -> 0%
where the time goes in v1:
time: 966 us; the launch traced here: 963 us
  waiting for transfers between devices  767 us (79%)
  starting transfers between devices  76.5 us (8%)
  other arithmetic  59.7 us (6%)
  matrix products  27.2 us (3%)
  local copies, waits for them, and re-layouts  17.7 us (2%)
  between operations  15 us (2%)
    psum x1, waiting for transfers between devices, on_device(): g_cols = lax.psum(jnp.dot(greens, col_hit, precision=highest), 'col')  629 us
    all_gather x1, waiting for transfers between devices, on_device(): lax.all_gather(jnp.dot(row_hit, greens, precision=highest), 'row')  111 us
    ppermute x2, starting transfers between devices, padded_2(): before = lax.ppermute(last, axis, up)  49.7 us
    another operation x6, other arithmetic, on_device(): lower_factor = jnp.linalg.cholesky(normal_matrix)  34.2 us
    ppermute x2, waiting for transfers between devices, from_behind(): return lax.ppermute(value, axis, pairs)  24 us
    ppermute x2, starting transfers between devices, padded_2(): after = lax.ppermute(leading, axis, down)  22.1 us
    another operation x3, other arithmetic, on_device(): lax.linalg.triangular_solve(lower_factor, middle, left_side=True, lower=T...  19.7 us
  transfers between devices with their start and end apart: 8, of which 6 were waited for; matrix products, arithmetic and copies ran while one was open for 0% of the time, Pallas kernels for 0%

profile of v1, /device:TPU:0, one launch (start us, length us, event | category | flops | bytes accessed | tf_op | source)
XLA Modules:
  0.0 963.1 jit_solution(754197896855138678)
XLA Ops:
  6.6 3.4 fusion.4
  10.1 2.6 convolution_bitcast_fusion
  12.6 110.9 %all-gather.3.cloned.1.call-done = f32[4096,432]{0,1:T(8,128)} async-done(((f32[256,432]{0,1:T(8,128)}), f32[4096,432]{0,1:T(8,128)}) %all-gather.3.cloned.1.call-update) | async-done | bytes 7077904 | tf_op jit(solution)/shard_map/all_gather | solution.py:84
  123.6 6.2 copy.29
  129.8 1.9 bitcast_reduce_fusion
  133.2 629.0 %all-reduce.4.cloned.1.call-done = (f32[864,256]{1,0:T(8,128)}, f32[256,256]{1,0:T(8,128)}) async-done(((f32[864,256]{1,0:T(8,128)}, f32[256,256]{1,0:T(8,128)}), (f32[864,256]{1,0:T(8,128)}, f32[256,256]{1,0:T(8,128)})) %all-reduce.4.cloned.1.call-update) | async-done | bytes 1146896 | tf_op jit(solution)/shard_map/psum | solution.py:83
  767.2 11.7 %cholesky.50 = f32[128,128]{1,0:T(8,128)S(1)} custom-call(f32[128,128]{1,0:T(8,128)S(1)} %cholesky.118), custom_call_target="Cholesky" | custom-call | tf_op jit(solution)/shard_map/jit(cholesky)/cholesky | solution.py:90
  779.0 9.8 %custom-call.16 = f32[1,128,128]{1,2,0:T(8,128)S(1)} custom-call(f32[1,128,128]{2,1,0:T(8,128)S(1)} %get-tuple-element.32), custom_call_target="InvertDiagBlocksLowerTriangular" | custom-call | tf_op jit(solution)/shard_map/jit(cholesky)/cholesky | solution.py:90
  791.0 11.9 %cholesky.105 = f32[128,128]{1,0:T(8,128)S(1)} custom-call(f32[128,128]{1,0:T(8,128)S(1)} %convolution_subtract_fusion.3), custom_call_target="Cholesky" | custom-call | tf_op jit(solution)/shard_map/jit(cholesky)/cholesky | solution.py:90
  804.9 3.9 while.1
  808.9 19.7 %custom-call.17 = f32[2,128,128]{1,2,0:T(8,128)S(1)} custom-call(f32[2,128,128]{2,1,0:T(8,128)S(1)} %get-tuple-element.12), custom_call_target="InvertDiagBlocksLowerTriangular" | custom-call | tf_op jit(solution)/shard_map/triangular_solve | solution.py:92
  833.0 2.7 convolution_subtract_fusion
  835.7 2.1 copy.24
  841.5 10.2 %collective-permute-start.3 = (f32[72,432]{1,0:T(8,128)S(1)}, f32[72,432]{1,0:T(8,128)S(1)}, u32[]{:S(2)}, u32[]{:S(2)}) collective-permute-start(f32[72,432]{1,0:T(8,128)S(1)} %get-tuple-element.26), channel_id=1, source_target_pairs={{32,0},{64,32},{96,64},{128,96},{160,128},{192,160},{224,192},{256... | collective-permute-start | bytes 373256 | tf_op jit(solution)/shard_map/ppermute | solution.py:18
  854.6 10.3 %collective-permute-done.1 = f32[144,144]{1,0:T(8,128)S(1)} collective-permute-done((f32[144,144]{1,0:T(8,128)S(1)}, f32[144,144]{1,0:T(8,128)S(1)}, u32[]{:S(2)}, u32[]{:S(2)}) %collective-permute-start.1) | collective-permute-done | bytes 82976 | tf_op jit(solution)/shard_map/ppermute | solution.py:26
  864.9 1.9 fusion
  867.0 2.0 copy.25
  869.0 3.1 fusion.50
  872.9 47.8 %collective-permute-start.4 = (f32[864,72]{0,1:T(8,128)}, f32[864,72]{0,1:T(8,128)}, u32[]{:S(2)}, u32[]{:S(2)}) collective-permute-start(f32[864,72]{0,1:T(8,128)} %get-tuple-element.27), channel_id=1, source_target_pairs={{0,1},{1,2},{2,3},{3,4},{4,5},{5,6},{6,7},{7,8},{8,9},{9,10},{10,1... | collective-permute-start | bytes 746504 | tf_op jit(solution)/shard_map/ppermute | solution.py:17
  920.8 11.9 %collective-permute-start.5 = (f32[864,72]{0,1:T(8,128)}, f32[864,72]{0,1:T(8,128)}, u32[]{:S(2)}, u32[]{:S(2)}) collective-permute-start(f32[864,72]{0,1:T(8,128)} %get-tuple-element.28), channel_id=1, source_target_pairs={{1,0},{2,1},{3,2},{4,3},{5,4},{6,5},{7,6},{8,7},{9,8},{10,9},{11,1... | collective-permute-start | bytes 746504 | tf_op jit(solution)/shard_map/ppermute | solution.py:18
  932.9 2.7 collective-permute-start
  935.6 2.4 collective-permute-done.5
  939.2 13.7 %collective-permute-done = f32[144,144]{0,1:T(8,128)S(1)} collective-permute-done((f32[144,144]{0,1:T(8,128)S(1)}, f32[144,144]{0,1:T(8,128)S(1)}, u32[]{:S(2)}, u32[]{:S(2)}) %collective-permute-start) | collective-permute-done | bytes 82976 | tf_op jit(solution)/shard_map/ppermute | solution.py:26
  952.9 2.1 fusion.6
  (67 shorter events, 28.0 us)
Async XLA Ops:
  6.5 831.3 %copy-start = (f32[6,144,144]{2,1,0:T(8,128)S(1)}, f32[6,144,144]{2,1,0:T(8,128)}, u32[]{:S(2)}) copy-start(f32[6,144,144]{2,1,0:T(8,128)} %param.10) | copy-start | bytes 1492996
  6.5 3.5 copy-start.1
  6.5 3.5 copy-start.6
  6.5 117.0 %all-gather.3.cloned.1.call-start = ((), (), s32[]{:S(2)}) async-start(), calls=%async_computation | async-start | bytes 7520256 | tf_op jit(solution)/shard_map/all_gather | solution.py:84
  10.0 752.2 %all-reduce.4.cloned.1.call-start = ((), (), s32[]{:S(2)}) async-start(), calls=%async_computation.1 | async-start | bytes 2293760 | tf_op jit(solution)/shard_map/psum | solution.py:83
  131.7 1.5 copy-start.7
  828.6 4.4 copy-start.3
  837.8 14.0 %copy-start.2 = (f32[6,144,144]{2,1,0:T(8,128)S(1)}, f32[6,144,144]{2,1,0:T(8,128)}, u32[]{:S(2)}) copy-start(f32[6,144,144]{2,1,0:T(8,128)} %param.11) | copy-start | bytes 1492996
  839.6 14.1 %collective-permute-start.2 = (f32[72,432]{1,0:T(8,128)S(1)}, f32[72,432]{1,0:T(8,128)S(1)}, u32[]{:S(2)}, u32[]{:S(2)}) collective-permute-start(f32[72,432]{1,0:T(8,128)S(1)} %get-tuple-element.25), channel_id=1, source_target_pairs={{0,32},{32,64},{64,96},{96,128},{128,160},{160,192},{192,224},{224... | collective-permute-start | bytes 373256 | tf_op jit(solution)/shard_map/ppermute | solution.py:17
  841.5 12.9 %collective-permute-start.3 = (f32[72,432]{1,0:T(8,128)S(1)}, f32[72,432]{1,0:T(8,128)S(1)}, u32[]{:S(2)}, u32[]{:S(2)}) collective-permute-start(f32[72,432]{1,0:T(8,128)S(1)} %get-tuple-element.26), channel_id=1, source_target_pairs={{32,0},{64,32},{96,64},{128,96},{160,128},{192,160},{224,192},{256... | collective-permute-start | bytes 373256 | tf_op jit(solution)/shard_map/ppermute | solution.py:18
  851.8 13.1 %collective-permute-start.1 = (f32[144,144]{1,0:T(8,128)S(1)}, f32[144,144]{1,0:T(8,128)S(1)}, u32[]{:S(2)}, u32[]{:S(2)}) collective-permute-start(f32[144,144]{1,0:T(8,128)S(1)} %slice_bitcast_fusion.1), channel_id=1, source_target_pairs={{0,32},{32,64},{64,96},{96,128},{128,160},{160,192},{192,224},{224... | collective-permute-start | bytes 248840 | tf_op jit(solution)/shard_map/ppermute | solution.py:26
  867.0 2.0 copy-start.4
  869.0 63.7 %copy-start.5 = (f32[3,144,144]{2,1,0:T(8,128)S(1)}, f32[3,144,144]{2,1,0:T(8,128)}, u32[]{:S(2)}) copy-start(f32[3,144,144]{2,1,0:T(8,128)} %param.13) | copy-start | bytes 746500
  872.9 62.7 %collective-permute-start.4 = (f32[864,72]{0,1:T(8,128)}, f32[864,72]{0,1:T(8,128)}, u32[]{:S(2)}, u32[]{:S(2)}) collective-permute-start(f32[864,72]{0,1:T(8,128)} %get-tuple-element.27), channel_id=1, source_target_pairs={{0,1},{1,2},{2,3},{3,4},{4,5},{5,6},{6,7},{7,8},{8,9},{9,10},{10,1... | collective-permute-start | bytes 746504 | tf_op jit(solution)/shard_map/ppermute | solution.py:17
  920.8 17.3 %collective-permute-start.5 = (f32[864,72]{0,1:T(8,128)}, f32[864,72]{0,1:T(8,128)}, u32[]{:S(2)}, u32[]{:S(2)}) collective-permute-start(f32[864,72]{0,1:T(8,128)} %get-tuple-element.28), channel_id=1, source_target_pairs={{1,0},{2,1},{3,2},{4,3},{5,4},{6,5},{7,6},{8,7},{9,8},{10,9},{11,1... | collective-permute-start | bytes 746504 | tf_op jit(solution)/shard_map/ppermute | solution.py:18
  932.9 20.0 %collective-permute-start = (f32[144,144]{0,1:T(8,128)S(1)}, f32[144,144]{0,1:T(8,128)S(1)}, u32[]{:S(2)}, u32[]{:S(2)}) collective-permute-start(f32[144,144]{0,1:T(8,128)S(1)} %slice_bitcast_fusion), channel_id=1, source_target_pairs={{0,1},{1,2},{2,3},{3,4},{4,5},{5,6},{6,7},{7,8},{8,9},{9,10},{10,1... | collective-permute-start | bytes 248840 | tf_op jit(solution)/shard_map/ppermute | solution.py:26
Sparse Core Ops, SparseCore 0:
  10.1 113.4 all-gather.2
  133.3 628.8 all-reduce.3
